TPU v7x, 512 devices: a whole 4x4x16 slice. The times are simulated.
512 devices in a mesh: noise: 16 (over x, z_lo), row: 32 (over z_hi, y, core).
Axes of the slice: x: 4, y: 4, z: 16 (z_hi: 4, z_lo: 4; z = z_hi * 4 + z_lo), core: 2. Of those that a mesh axis runs over, the one named last changes fastest.
Arguments:
- activations: bfloat16 [64, 2048, 768], P('noise', 'row'), may hold values from -6 to 6
- cond_scale: bfloat16 [64, 2048, 768], P('noise', 'row'), may hold values from 0.25 to 16
- cond_shift: bfloat16 [64, 2048, 768], P('noise', 'row'), may hold values from -4 to 4
- output_gate: bfloat16 [64, 2048, 768], P('noise', 'row'), may hold values from -8 to 8
- pair_repr: bfloat16 [2048, 2048, 128], P('row', 'noise'), may hold values from -6 to 6
- bias_weight: bfloat16 [128, 8], replicated, may hold values from -1.5 to 1.5
- query_weight: bfloat16 [768, 384], P('noise'), may hold values from -0.21875 to 0.21875
- query_bias: bfloat16 [384], replicated, may hold values from -4 to 4
- key_weight: bfloat16 [768, 384], P('noise'), may hold values from -0.21875 to 0.21875
- value_weight: bfloat16 [768, 384], P('noise'), may hold values from -0.21875 to 0.21875
- output_weight: bfloat16 [384, 768], P('noise'), may hold values from -0.3125 to 0.3125
- token_mask: int32 [64, 2048], P('noise', 'row'), may hold values from 0 to 1, as said below
Outputs:
- updated: bfloat16 [64, 2048, 768], P('noise', 'row')
Inputs may be any that keep to these rules, and one draw needn't show every extreme that they name: `token_mask`: in each sample the tokens with mask 1 form a prefix of half of 2048 tokens or more, and some sample has all 2048 tokens.
All inputs are finite; a program needn't handle non-finite values.
Results may differ from a plain program's by a relative error of at most 0.012.
The roundings to bfloat16 on the way count: a program that leaves them out, or rounds other values in their place, can miss the bound.
Values may be sent and summed in bfloat16 or wider, within the bound.
A program may use at most 128 MiB of HBM per device.

v0:
```python
import math

import jax
import jax.numpy as jnp
from jax import lax
from jax.sharding import PartitionSpec as P

epsilon = 1e-05
masked_score = -1e30


def layer_norm(tensor):
    average = jnp.mean(tensor, axis=-1, keepdims=True)
    centred = tensor - average
    variance = jnp.mean(centred * centred, axis=-1, keepdims=True)
    return centred * lax.rsqrt(variance + epsilon)


def body(
    activations,
    cond_scale,
    cond_shift,
    output_gate,
    pair_repr,
    bias_weight,
    query_weight,
    query_bias,
    key_weight,
    value_weight,
    output_weight,
    token_mask,
):
    samples_here, rows_here, features = activations.shape
    head_count = bias_weight.shape[1]
    head_features = query_weight.shape[1]
    head_width = head_features // head_count
    score_factor = 1.0 / math.sqrt(head_width)
    query_full, key_full, value_full, output_full = (
        lax.all_gather(query_weight, "noise", axis=0, tiled=True),
        lax.all_gather(key_weight, "noise", axis=0, tiled=True),
        lax.all_gather(value_weight, "noise", axis=0, tiled=True),
        lax.all_gather(output_weight, "noise", axis=0, tiled=True),
    )
    normed = layer_norm(activations.astype(jnp.float32))
    shifted = (cond_scale.astype(jnp.float32) * normed + cond_shift.astype(jnp.float32)).astype(
        jnp.bfloat16
    )
    flat_rows = shifted.reshape(samples_here * rows_here, features)
    queries = (
        jnp.dot(flat_rows, query_full, preferred_element_type=jnp.float32)
        + query_bias.astype(jnp.float32)
    ).astype(jnp.bfloat16)
    key_rows = jnp.dot(flat_rows, key_full, preferred_element_type=jnp.float32).astype(jnp.bfloat16)
    value_rows = jnp.dot(flat_rows, value_full, preferred_element_type=jnp.float32).astype(
        jnp.bfloat16
    )
    queries = queries.reshape(samples_here, rows_here, head_features)
    key_rows = key_rows.reshape(samples_here, rows_here, head_features)
    value_rows = value_rows.reshape(samples_here, rows_here, head_features)
    key_valid = token_mask.astype(jnp.bfloat16)
    pair_normed = layer_norm(pair_repr.astype(jnp.float32))
    bias_tile = jnp.einsum(
        "ijc,ch->hij", pair_normed, bias_weight.astype(jnp.float32), precision=lax.Precision.HIGHEST
    ).astype(jnp.bfloat16)
    bias_band = lax.all_gather(bias_tile, "noise", axis=2, tiled=True)
    query_heads = queries.reshape(samples_here, rows_here, head_count, head_width)
    running_max = jnp.full((samples_here, head_count, rows_here), -jnp.inf, jnp.float32)
    running_sum = jnp.zeros((samples_here, head_count, rows_here), jnp.float32)
    accumulated = jnp.zeros((samples_here, head_count, rows_here, head_width), jnp.float32)
    key_piece = lax.all_gather(key_rows, "row", axis=1, tiled=True)
    value_piece = lax.all_gather(value_rows, "row", axis=1, tiled=True)
    valid_piece = lax.all_gather(key_valid, "row", axis=1, tiled=True)
    piece_rows = key_piece.shape[1]
    key_heads = key_piece.reshape(samples_here, piece_rows, head_count, head_width)
    value_heads = value_piece.reshape(samples_here, piece_rows, head_count, head_width)
    bias_piece = bias_band.astype(jnp.float32)
    scores = (
        jnp.einsum("sihd,sjhd->shij", query_heads, key_heads, preferred_element_type=jnp.float32)
        * score_factor
        + bias_piece[None]
    )
    scores = jnp.where(valid_piece[:, None, None, :] > 0, scores, masked_score)
    updated_max = jnp.max(scores, axis=-1)
    factor = jnp.exp(running_max - updated_max)
    weights = jnp.exp(scores - updated_max[..., None])
    running_sum = running_sum * factor + jnp.sum(weights, axis=-1)
    accumulated = accumulated * factor[..., None] + jnp.einsum(
        "shij,sjhd->shid",
        weights.astype(jnp.bfloat16),
        value_heads,
        preferred_element_type=jnp.float32,
    )
    mixture = accumulated / running_sum[..., None]
    attended = (
        mixture.transpose(0, 2, 1, 3)
        .reshape(samples_here, rows_here, head_features)
        .astype(jnp.bfloat16)
    )
    projected = jnp.dot(
        attended.reshape(samples_here * rows_here, head_features),
        output_full,
        preferred_element_type=jnp.float32,
    ).reshape(samples_here, rows_here, features)
    return (
        activations.astype(jnp.float32)
        + jax.nn.sigmoid(output_gate.astype(jnp.float32)) * projected
    ).astype(jnp.bfloat16)


def solution(mesh):
    return jax.shard_map(
        body,
        mesh=mesh,
        in_specs=(
            P("noise", "row", None),
            P("noise", "row", None),
            P("noise", "row", None),
            P("noise", "row", None),
            P("row", "noise", None),
            P(),
            P("noise", None),
            P(),
            P("noise", None),
            P("noise", None),
            P("noise", None),
            P("noise", "row"),
        ),
        out_specs=P("noise", "row", None),
        check_vma=False,
    )
```

profile of v0, /device:TPU:1, one launch (start us, length us, event | category | flops | bytes accessed | tf_op | source)
XLA Modules:
  0.0 390.0 jit_solution(16651615040873684399)
XLA Ops:
  6.6 0.0 all-gather.7.cloned.1.call-start
  6.6 2.3 convert_reduce_fusion
  8.9 3.6 fusion.8
  12.6 5.5 %fusion.25 = bf16[8,64,128]{2,0,1:T(8,128)(2,1)} fusion(bf16[64,128,128]{2,1,0:T(8,128)(2,1)} %param.16, f32[64,128]{1,0:T(8,128)S(1)} %add_rsqrt_fusion, f32[64,128]{1,0:T(8,128)S(1)} %broadcast_multiply_fusion, bf16[128,8]{0,1:T(8,128)(2,1)S(1)} %copy-done), kind=kOutput, calls=%fused_computation.27 | convolution fusion | flops 103874560 | bytes 2295808 | tf_op jit(solution)/shard_map/ijc,ch->hij/dot_general | solution.py:62
  18.1 0.0 all-gather.7.cloned.1.call-update
  18.1 0.0 all-gather.5.cloned.1.call-start
  18.2 0.1 convert_reduce_fusion.1
  18.3 0.2 fusion.36
  18.6 0.3 fusion.39
  18.9 44.1 %all_gather.26 = bf16[768,384]{1,0:T(8,128)(2,1)S(1)} all-gather(bf16[48,384]{1,0:T(8,128)(2,1)S(1)} %copy-done.8), channel_id=1, replica_groups=mesh['noise'=16,'row'=32] {'noise'}, dimensions={0}, use_global_device_ids=true | all-gather | bytes 626688 | tf_op jit(solution)/shard_map/all_gather | solution.py:40
  63.0 1.0 convolution_convert_fusion.1
  64.1 0.0 all-gather.5.cloned.1.call-update
  64.1 0.0 all-gather.9.cloned.1.call-start
  64.2 41.9 %all_gather.29 = bf16[768,384]{1,0:T(8,128)(2,1)S(1)} all-gather(bf16[48,384]{1,0:T(8,128)(2,1)S(1)} %copy-done.9), channel_id=1, replica_groups=mesh['noise'=16,'row'=32] {'noise'}, dimensions={0}, use_global_device_ids=true | all-gather | bytes 626688 | tf_op jit(solution)/shard_map/all_gather | solution.py:41
  106.1 1.0 convolution_convert_fusion
  107.1 0.0 all-gather.9.cloned.1.call-update
  107.2 36.7 %all_gather.25 = bf16[768,384]{1,0:T(8,128)(2,1)S(1)} all-gather(bf16[48,384]{1,0:T(8,128)(2,1)S(1)} %copy-done.10), channel_id=1, replica_groups=mesh['noise'=16,'row'=32] {'noise'}, dimensions={0}, use_global_device_ids=true | all-gather | bytes 626688 | tf_op jit(solution)/shard_map/all_gather | solution.py:39
  143.9 0.4 fusion.21
  144.3 1.3 reshape.72
  145.6 94.3 %all-gather = bf16[32,64,4]{1,2,0:T(4,128)(2,1)S(1)} all-gather(bf16[1,64,4]{1,2,0:T(4,128)(2,1)S(1)} %convert_bitcast_fusion), channel_id=1, replica_groups=mesh['noise'=16,'row'=32] {'row'}, dimensions={0}, use_global_device_ids=true | all-gather | bytes 16896 | tf_op jit(solution)/shard_map/all_gather | solution.py:72
  239.9 0.1 reshape.69
  240.0 41.1 %all_gather.31 = bf16[384,768]{1,0:T(8,128)(2,1)} all-gather(bf16[24,768]{1,0:T(8,128)(2,1)S(1)} %copy-done.11), channel_id=1, replica_groups=mesh['noise'=16,'row'=32] {'noise'}, dimensions={0}, use_global_device_ids=true | all-gather | bytes 626688 | tf_op jit(solution)/shard_map/all_gather | solution.py:42
  281.1 4.7 %copy.29 = f32[8,64,2048]{2,1,0:T(8,128)} copy(bf16[8,64,2048]{2,0,1:T(8,128)(2,1)} %all-gather.7.cloned.1.call-done) | data formatting | bytes 6291456 | tf_op jit(solution)/shard_map/convert_element_type | solution.py:76
  285.8 8.6 %copy.27 = bf16[4,2048,384]{1,2,0:T(8,128)(2,1)} copy(bf16[4,2048,384]{2,1,0:T(8,128)(2,1)} %all-gather.5.cloned.1.call-done) | data formatting | bytes 12582912 | tf_op jit(solution)/shard_map/all_gather | solution.py:70
  294.5 6.6 %fusion.2 = (f32[4,8,64]{2,1,0:T(8,128)S(1)}, f32[4,8,64,2048]{3,2,1,0:T(8,128)S(1)}) fusion(f32[8,64,2048]{2,1,0:T(8,128)} %copy.29, pred[4,2048]{1,0:T(4,128)(4,1)S(1)} %bitcast.51, bf16[4,2048,8,48]{1,3,2,0:T(8,128)(2,1)} %bitcast.44, bf16[4,64,8,48]{3,2,1,0:T(8,128)(2,1)} %reshape.72), kind=kOutput, calls=%fused_computation.4 | convolution fusion | flops 419428352 | bytes 27475968 | tf_op jit(solution)/shard_map/sihd,sjhd->shij/dot_general | solution.py:78
  301.1 0.7 multiply_bitcast_fusion
  301.8 4.7 %fusion = f32[4,8,64]{2,1,0:T(8,128)S(1)} fusion(f32[4,8,64,2048]{3,2,1,0:T(8,128)S(1)} %get-tuple-element.6, f32[4,8,64]{2,1,0:T(8,128)S(1)} %get-tuple-element.5, f32[8,64,2048]{2,1,0:T(8,128)S(1)} %copy-done.1, pred[4,2048]{1,0:T(4,128)(4,1)S(1)} %bitcast.52), kind=kLoop, calls=%fused_computation.2 | loop fusion | flops 20969472 | bytes 20996096 | tf_op jit(solution)/shard_map/reduce_sum | solution.py:86
  306.4 0.4 copy-done.2
  306.9 55.0 %all-gather.9.cloned.1.call-done = bf16[4,2048,384]{2,1,0:T(8,128)(2,1)} async-done(((bf16[4,64,384]{2,1,0:T(8,128)(2,1)}), bf16[4,2048,384]{2,1,0:T(8,128)(2,1)}) %all-gather.9.cloned.1.call-update) | async-done | bytes 6291472 | tf_op jit(solution)/shard_map/all_gather | solution.py:71
  361.9 8.6 %copy.30 = bf16[4,2048,384]{1,2,0:T(8,128)(2,1)} copy(bf16[4,2048,384]{2,1,0:T(8,128)(2,1)} %all-gather.9.cloned.1.call-done) | data formatting | bytes 12582912 | tf_op jit(solution)/shard_map/all_gather | solution.py:71
  370.5 11.7 %fusion.31 = bf16[4,64,8,48]{1,3,2,0:T(8,128)(2,1)S(1)} fusion(bf16[4,2048,8,48]{1,3,2,0:T(8,128)(2,1)} %bitcast.45, f32[4,8,64,2048]{3,2,1,0:T(8,128)} %copy-done.2, f32[4,8,64]{2,1,0:T(8,128)S(1)} %get-tuple-element.5, f32[8,64,2048]{2,1,0:T(8,128)} %copy.29, pred[4,2048]{1,0:T(4,128)(4,1)S(1)} %bitcast.53, f32[4,64,8]{1,2,0:T(8,128)S(1)} %bitcast_add_fusion, ...), kind=kOutput, calls=%fused_computation.29 | convolution fusion | flops 423919616 | bytes 27492352 | tf_op jit(solution)/shard_map/shij,sjhd->shid/dot_general | solution.py:87
  382.3 1.2 fusion.20
  (42 shorter events, 0.2 us)
Async XLA Ops:
  6.5 6.0 %copy-start = (bf16[128,8]{0,1:T(8,128)(2,1)S(1)}, bf16[128,8]{0,1:T(8,128)(2,1)}, u32[]{:S(2)}) copy-start(bf16[128,8]{0,1:T(8,128)(2,1)} %param.17) | copy-start | bytes 6148
  6.5 11.6 %copy-start.3 = (bf16[4,64,768]{2,1,0:T(8,128)(2,1)S(1)}, bf16[4,64,768]{2,1,0:T(8,128)(2,1)}, u32[]{:S(2)}) copy-start(bf16[4,64,768]{2,1,0:T(8,128)(2,1)} %param.12) | copy-start | bytes 1179652
  6.5 12.0 %copy-start.7 = (bf16[4,64,768]{2,1,0:T(8,128)(2,1)S(1)}, bf16[4,64,768]{2,1,0:T(8,128)(2,1)}, u32[]{:S(2)}) copy-start(bf16[4,64,768]{2,1,0:T(8,128)(2,1)} %param.13) | copy-start | bytes 1179652
  6.5 12.0 %copy-start.6 = (bf16[4,64,768]{2,1,0:T(8,128)(2,1)S(1)}, bf16[4,64,768]{2,1,0:T(8,128)(2,1)}, u32[]{:S(2)}) copy-start(bf16[4,64,768]{2,1,0:T(8,128)(2,1)} %param.14) | copy-start | bytes 1179652
  6.5 12.4 %copy-start.8 = (bf16[48,384]{1,0:T(8,128)(2,1)S(1)}, bf16[48,384]{1,0:T(8,128)(2,1)}, u32[]{:S(2)}) copy-start(bf16[48,384]{1,0:T(8,128)(2,1)} %param.20) | copy-start | bytes 110596
  6.5 57.6 %copy-start.9 = (bf16[48,384]{1,0:T(8,128)(2,1)S(1)}, bf16[48,384]{1,0:T(8,128)(2,1)}, u32[]{:S(2)}) copy-start(bf16[48,384]{1,0:T(8,128)(2,1)} %param.21) | copy-start | bytes 110596
  6.6 274.5 %all-gather.7.cloned.1.call-start = ((), (), s32[]{:S(2)}) async-start(), calls=%async_computation.1 | async-start | bytes 2228224 | tf_op jit(solution)/shard_map/all_gather | solution.py:65
  8.9 98.2 %copy-start.14 = (bf16[384]{0:T(512)(128)(2,1)S(1)}, bf16[384]{0:T(512)(128)(2,1)}, u32[]{:S(2)}) copy-start(bf16[384]{0:T(512)(128)(2,1)} %param.19) | copy-start | bytes 2308
  8.9 98.2 %copy-start.10 = (bf16[48,384]{1,0:T(8,128)(2,1)S(1)}, bf16[48,384]{1,0:T(8,128)(2,1)}, u32[]{:S(2)}) copy-start(bf16[48,384]{1,0:T(8,128)(2,1)} %param.18) | copy-start | bytes 110596
  12.5 133.0 %copy-start.13 = (s32[4,64]{1,0:T(4,128)S(1)}, s32[4,64]{1,0:T(4,128)}, u32[]{:S(2)}) copy-start(s32[4,64]{1,0:T(4,128)} %param.23) | copy-start | bytes 3076
  12.5 227.4 %copy-start.11 = (bf16[24,768]{1,0:T(8,128)(2,1)S(1)}, bf16[24,768]{1,0:T(8,128)(2,1)}, u32[]{:S(2)}) copy-start(bf16[24,768]{1,0:T(8,128)(2,1)} %param.22) | copy-start | bytes 110596
  18.1 267.7 %all-gather.5.cloned.1.call-start = ((), (), s32[]{:S(2)}) async-start(), calls=%async_computation | async-start | bytes 6488064 | tf_op jit(solution)/shard_map/all_gather | solution.py:70
  64.1 297.8 %all-gather.9.cloned.1.call-start = ((), (), s32[]{:S(2)}) async-start(), calls=%async_computation.2 | async-start | bytes 6488064 | tf_op jit(solution)/shard_map/all_gather | solution.py:71
  294.5 7.3 %copy-start.1 = (f32[8,64,2048]{2,1,0:T(8,128)S(1)}, f32[8,64,2048]{2,1,0:T(8,128)}, u32[]{:S(2)}) copy-start(f32[8,64,2048]{2,1,0:T(8,128)} %copy.29) | copy-start | bytes 12582916
  301.1 5.7 %copy-start.2 = (f32[4,8,64,2048]{3,2,1,0:T(8,128)}, f32[4,8,64,2048]{3,2,1,0:T(8,128)S(1)}, u32[]{:S(2)}) copy-start(f32[4,8,64,2048]{3,2,1,0:T(8,128)S(1)} %get-tuple-element.6) | copy-start | bytes 50331652
  306.8 63.7 %copy-start.12 = (f32[4,64,8]{1,2,0:T(8,128)S(1)}, f32[4,64,8]{1,2,0:T(8,128)}, u32[]{:S(2)}) copy-start(f32[4,64,8]{1,2,0:T(8,128)} %multiply_bitcast_fusion) | copy-start | bytes 24580
  370.5 11.8 %copy-start.4 = (bf16[4,64,768]{2,1,0:T(8,128)(2,1)S(1)}, bf16[4,64,768]{2,1,0:T(8,128)(2,1)}, u32[]{:S(2)}) copy-start(bf16[4,64,768]{2,1,0:T(8,128)(2,1)} %param.12) | copy-start | bytes 1179652
  370.5 11.8 %copy-start.5 = (bf16[384,768]{1,0:T(8,128)(2,1)S(1)}, bf16[384,768]{1,0:T(8,128)(2,1)}, u32[]{:S(2)}) copy-start(bf16[384,768]{1,0:T(8,128)(2,1)} %all_gather.31) | copy-start | bytes 1769476
  370.5 11.8 %copy-start.15 = (bf16[4,64,768]{2,1,0:T(8,128)(2,1)S(1)}, bf16[4,64,768]{2,1,0:T(8,128)(2,1)}, u32[]{:S(2)}) copy-start(bf16[4,64,768]{2,1,0:T(8,128)(2,1)} %param.15) | copy-start | bytes 1179652
Sparse Core Ops, SparseCore 0:
  18.2 97.1 all-gather.6
  118.6 125.4 all-gather.4
  247.3 114.5 all-gather.8
where the time goes:
time: 391 us; the launch traced here: 390 us
  blocking collectives  258 us (66%)
  waiting for transfers between devices  55.1 us (14%)
  matrix products  27.5 us (7%)
  local copies, waits for them, and re-layouts  23.8 us (6%)
  between operations  13.4 us (3%)
  other arithmetic  12 us (3%)
    all_gather x1, blocking collectives, body(): valid_piece = lax.all_gather(key_valid, 'row', axis=1, tiled=True)  94.3 us
    all_gather x1, waiting for transfers between devices, body(): value_piece = lax.all_gather(value_rows, 'row', axis=1, tiled=True)  55 us
    all_gather x1, blocking collectives, body(): lax.all_gather(key_weight, 'noise', axis=0, tiled=True)  44.1 us
    all_gather x1, blocking collectives, body(): lax.all_gather(value_weight, 'noise', axis=0, tiled=True)  41.9 us
    all_gather x1, blocking collectives, body(): lax.all_gather(output_weight, 'noise', axis=0, tiled=True)  41.1 us
    all_gather x1, blocking collectives, body(): lax.all_gather(query_weight, 'noise', axis=0, tiled=True)  36.7 us
    dot_general x1, matrix products, body(): jnp.einsum('shij,sjhd->shid', weights.astype(jnp.bfloat16), value_heads,...  11.7 us
    all_gather x1, local copies, waits for them, and re-layouts, body(): value_piece = lax.all_gather(value_rows, 'row', axis=1, tiled=True)  8.63 us
  transfers between devices with their start and end apart: 3, of which 1 were waited for; matrix products, arithmetic and copies ran while one was open for 8% of the time, Pallas kernels for 0%

commit v1 on v0

v1 whole, which is shorter than its diff:
```python
import functools
import math

import jax
import jax.numpy as jnp
from jax import lax
from jax.experimental import pallas as pl
from jax.experimental.pallas import tpu as pltpu
from jax.sharding import PartitionSpec as P

MESH = pl.DeviceIdType.MESH
f32 = jnp.float32
bf16 = jnp.bfloat16
epsilon = 1e-05
masked_score = -1e30
LOG2E = math.log2(math.e)

S = 4
T = 64
D = 768
F = 384
HW = 48
HALF = 192
WC = 640
KEYS = 2048
NT = (((1,), (1,)), ((), ()))


def iota(shape, dim):
    return lax.broadcasted_iota(jnp.int32, shape, dim)


def layer_norm(tensor):
    average = jnp.mean(tensor, axis=-1, keepdims=True)
    centred = tensor - average
    variance = jnp.mean(centred * centred, axis=-1, keepdims=True)
    return centred * lax.rsqrt(variance + epsilon)


def kernel(
    act_h, scale_h, shift_h, gate_h, pair_h, wb_ref, wq_ref, qb_ref, wk_ref, wv_ref, wo_ref, mask_ref,
    out_ref,
    act, scale, shift, gate, pair, local_sem,
    wg, wog, wop, qrow,
    sh, kvs, kvg, qs, qg,
    bt, btb, bc, bg, bf,
    mk, mks, mko, mg, mb,
    kaug, vaug, qaug,
    os_, og, xs, at,
    w_zl, w_x, wo_zl, wo_x, c_sem, b_zh, b_zl, b_x, m_zh, m_y, k_zh, q_zh, k_y, o_zh, a_c,
):
    noise, row = lax.axis_index("noise"), lax.axis_index("row")
    x, zl = noise // 4, lax.rem(noise, 4)
    zh, y, core = row // 8, lax.rem(row // 2, 4), lax.rem(row, 2)
    other = 1 - core

    def turn(v, d):
        return lax.rem(v + d + 4, 4)

    def dev(x=x, zl=zl, zh=zh, y=y, core=core):
        return (x * 4 + zl, zh * 8 + y * 2 + core)

    def remote(src, dst, sems, device):
        return pltpu.make_async_remote_copy(
            src_ref=src, dst_ref=dst, send_sem=sems[0], recv_sem=sems[1], device_id=device, device_id_type=MESH
        )

    def pair_of(sem, *index):
        return sem.at[(0, *index)], sem.at[(1, *index)]

    barrier = pltpu.get_barrier_semaphore()
    for d in (1, 2, 3):
        for where in (dev(zh=turn(zh, d)), dev(zl=turn(zl, d)), dev(x=turn(x, d)), dev(y=turn(y, d))):
            pl.semaphore_signal(barrier, inc=1, device_id=where, device_id_type=MESH)
    pl.semaphore_signal(barrier, inc=1, device_id=dev(core=other), device_id_type=MESH)

    loads = [
        pltpu.make_async_copy(source, target, local_sem.at[i])
        for i, (source, target) in enumerate(
            ((pair_h, pair), (act_h, act), (scale_h, scale), (shift_h, shift), (gate_h, gate))
        )
    ]
    for load in loads:
        load.start()

    def chosen(first):
        return ((iota((F, WC), 0) == iota((F, WC), 1) - first + HALF * core)
                & (iota((F, WC), 1) >= first) & (iota((F, WC), 1) < first + HALF)).astype(f32).astype(bf16)

    weights = (
        jnp.dot(wk_ref[...], chosen(0), preferred_element_type=f32)
        + jnp.dot(wv_ref[...], chosen(HALF), preferred_element_type=f32)
        + jnp.dot(wq_ref[...], chosen(2 * HALF), preferred_element_type=f32)
    )
    qrow[...] = jnp.dot(
        jnp.broadcast_to(qb_ref[...].astype(f32), (16, F)).astype(bf16), chosen(2 * HALF), preferred_element_type=f32
    )
    wg[noise] = weights.astype(bf16)
    wo = wo_ref[...].astype(f32)
    wog[noise] = jnp.concatenate([wo[:, :F], wo[:, F:]], axis=0).astype(bf16)
    lanes = (iota((T, 128), 1) == iota((T, 128), 0) + T * core).astype(f32).astype(bf16)
    mk[...] = jnp.zeros_like(mk)
    mk[0:S] = jnp.dot(mask_ref[...].astype(f32).astype(bf16), lanes, preferred_element_type=f32)
    mks[...] = mk[...].astype(bf16)

    pl.semaphore_wait(barrier, 13)

    w_zl_copies = [
        remote(wg.at[noise], wg.at[noise], pair_of(w_zl, d - 1), dev(zl=turn(zl, d))) for d in (1, 2, 3)
    ]
    for copy in w_zl_copies:
        copy.start()
    mask_core = remote(mks, mko, pair_of(c_sem, 0), dev(core=other))
    mask_core.start()

    wb = jnp.concatenate([wb_ref[...].astype(f32), jnp.zeros((128, 120), f32)], axis=1)
    wsum = jnp.sum(wb, axis=0, keepdims=True)
    wide = jnp.concatenate([wb, jnp.full((128, 128), 1.0 / 128, f32)], axis=1).astype(bf16)
    mean_at = jnp.where(iota((128, 128), 1) == 8, 1.0 / 128, 0.0).astype(bf16)
    loads[0].wait()

    def pair_rows(step, _):
        tile = pair[pl.ds(step * 8, 8)].reshape(1024, 128)
        both = jnp.dot(tile, wide, preferred_element_type=f32)
        mean = both[:, 128:]
        centred = tile.astype(f32) - mean
        square = (centred * centred).astype(bf16)
        table = both[:, :128] - mean * wsum + jnp.dot(square, mean_at, preferred_element_type=f32)
        for i in range(8):
            flipped = table[i * 128 : (i + 1) * 128].T
            bias = flipped[0:8] * lax.rsqrt(flipped[8:9] + epsilon)
            bt[:, pl.ds(step * 8 + i, 1), :] = bias.reshape(8, 1, 128)
        return 0

    lax.fori_loop(0, 8, pair_rows, 0)
    btb[...] = bt[...].astype(bf16).reshape(2, 4, T, 128)
    here = pl.ds(pl.multiple_of(core * T, T), T)
    bias_core = remote(btb.at[other], bc.at[:, here], pair_of(c_sem, 1), dev(core=other))
    bias_core.start()
    bc[:, here] = btb[core]

    for load in loads[1:4]:
        load.wait()

    def norm_rows(s, _):
        normed = layer_norm(act[s].astype(f32))
        sh[s, here] = (scale[s].astype(f32) * normed + shift[s].astype(f32)).astype(bf16)
        return 0

    lax.fori_loop(0, S, norm_rows, 0)
    shifted_core = remote(sh.at[:, here], sh.at[:, here], pair_of(c_sem, 2), dev(core=other))
    shifted_core.start()

    def weights_x(zl_from):
        block = x * 4 + zl_from
        copies = []
        for d in (1, 2, 3):
            copies.append(remote(wg.at[block], wg.at[block], pair_of(w_x, d - 1, zl_from), dev(x=turn(x, d))))
            copies[-1].start()
        return copies

    w_x_copies = weights_x(zl)
    for d in (1, 2, 3):
        source = turn(zl, -d)
        slot = wg.at[x * 4 + source]
        remote(slot, slot, pair_of(w_zl, d - 1), dev(zl=source)).wait_recv()
        w_x_copies += weights_x(source)

    there = pl.ds(pl.multiple_of(other * T, T), T)
    remote(btb.at[other], bc.at[:, there], pair_of(c_sem, 1), dev(core=other)).wait_recv()
    b_zh_copies = []
    for d in (1, 2, 3):
        to = turn(zh, d)
        b_zh_copies.append(remote(bc.at[to], bg.at[noise, zh], pair_of(b_zh, d - 1), dev(zh=to)))
        b_zh_copies[-1].start()
    bg[noise, zh] = bc[zh]
    mask_core.wait_recv()
    mg[y, zh] = mks[...] + mko[...]
    m_zh_copies = []
    for d in (1, 2, 3):
        m_zh_copies.append(remote(mg.at[y, zh], mg.at[y, zh], pair_of(m_zh, d - 1), dev(zh=turn(zh, d))))
        m_zh_copies[-1].start()
    wo_zl_copies = [
        remote(wog.at[noise], wog.at[noise], pair_of(wo_zl, d - 1), dev(zl=turn(zl, d))) for d in (1, 2, 3)
    ]
    for copy in wo_zl_copies:
        copy.start()

    def bias_x(zl_from):
        block = x * 4 + zl_from
        copies = []
        for d in (1, 2, 3):
            copies.append(remote(bg.at[block], bg.at[block], pair_of(b_x, d - 1, zl_from), dev(x=turn(x, d))))
            copies[-1].start()
        return copies

    for d in (1, 2, 3):
        source = turn(zh, -d)
        remote(bc.at[0], bg.at[noise, source], pair_of(b_zh, d - 1), dev(zh=source)).wait_recv()
    b_zl_copies = [
        remote(bg.at[noise], bg.at[noise], pair_of(b_zl, d - 1), dev(zl=turn(zl, d))) for d in (1, 2, 3)
    ]
    for copy in b_zl_copies:
        copy.start()
    b_x_copies = bias_x(zl)

    for d in (1, 2, 3):
        source = turn(zh, -d)
        slot = mg.at[y, source]
        remote(slot, slot, pair_of(m_zh, d - 1), dev(zh=source)).wait_recv()
    m_y_copies = []
    for d in (1, 2, 3):
        m_y_copies.append(remote(mg.at[y], mg.at[y], pair_of(m_y, d - 1), dev(y=turn(y, d))))
        m_y_copies[-1].start()

    remote(sh.at[:, there], sh.at[:, there], pair_of(c_sem, 2), dev(core=other)).wait_recv()
    for zl_from in range(4):
        for d in (1, 2, 3):
            slot = wg.at[turn(x, -d) * 4 + zl_from]
            remote(slot, slot, pair_of(w_x, d - 1, zl_from), dev(x=turn(x, -d))).wait_recv()

    def kv_copy(s, d):
        to = turn(zh, d)
        return remote(kvs.at[s, to], kvg.at[s, y, zh], pair_of(k_zh, s, d - 1), dev(zh=to))

    def q_copy(s, d):
        to = turn(zh, d)
        return remote(qs.at[s, to], qg.at[s, zh], pair_of(q_zh, s, d - 1), dev(zh=to))

    def project(s, _):
        rows = jnp.dot(sh[s], wg[...].reshape(D, WC), preferred_element_type=f32) + qrow[0:1]
        flipped = rows.T.astype(bf16)
        for h in range(4):
            kvs[s, h, 0:HW] = flipped[h * HW : (h + 1) * HW]
            kvs[s, h, HW : 2 * HW] = flipped[HALF + h * HW : HALF + (h + 1) * HW]
            qs[s, h] = flipped[2 * HALF + h * HW : 2 * HALF + (h + 1) * HW]
        for d in (1, 2, 3):
            kv_copy(s, d).start()
        for d in (1, 2, 3):
            q_copy(s, d).start()
        kvg[s, y, zh] = kvs[s, zh]
        qg[s, zh] = qs[s, zh]
        return 0

    lax.fori_loop(0, S, project, 0)

    def wo_x_send(zl_from):
        block = x * 4 + zl_from
        copies = []
        for d in (1, 2, 3):
            copies.append(remote(wog.at[block], wog.at[block], pair_of(wo_x, d - 1, zl_from), dev(x=turn(x, d))))
            copies[-1].start()
        return copies

    for d in (1, 2, 3):
        source = turn(zl, -d)
        slot = bg.at[x * 4 + source]
        remote(slot, slot, pair_of(b_zl, d - 1), dev(zl=source)).wait_recv()
        b_x_copies += bias_x(source)
    wo_x_copies = wo_x_send(zl)
    for d in (1, 2, 3):
        source = turn(zl, -d)
        slot = wog.at[x * 4 + source]
        remote(slot, slot, pair_of(wo_zl, d - 1), dev(zl=source)).wait_recv()
        wo_x_copies += wo_x_send(source)

    def ky_copy(s, d):
        return remote(kvg.at[s, y], kvg.at[s, y], pair_of(k_y, s, d - 1), dev(y=turn(y, d)))

    def forward(s):
        for d in (1, 2, 3):
            source = turn(zh, -d)
            remote(kvs.at[s, 0], kvg.at[s, y, source], pair_of(k_zh, s, d - 1), dev(zh=source)).wait_recv()
        for d in (1, 2, 3):
            ky_copy(s, d).start()

    forward(0)

    for d in (1, 2, 3):
        source = turn(y, -d)
        remote(mg.at[source], mg.at[source], pair_of(m_y, d - 1), dev(y=source)).wait_recv()
    for b in range(16):
        tokens = mg[b % 4, b // 4].astype(f32)
        for s in range(S):
            line = (tokens[s : s + 1] - 1.0) * (-masked_score)
            mb[s, :, b * 128 : (b + 1) * 128] = jnp.where(
                iota((16, 128), 0) == 0, jnp.broadcast_to(line, (16, 128)), 0.0
            ).astype(bf16)
    kaug[112:128] = jnp.zeros((16, KEYS), bf16)
    vaug[HW:128] = jnp.where(iota((80, KEYS), 0) == 0, 1.0, 0.0).astype(bf16)

    for zl_from in range(4):
        for d in (1, 2, 3):
            slot = bg.at[turn(x, -d) * 4 + zl_from]
            remote(slot, slot, pair_of(b_x, d - 1, zl_from), dev(x=turn(x, -d))).wait_recv()

    def widen(b, _):
        columns = pl.ds(pl.multiple_of(b * 128, 128), 128)
        bf[:, columns] = bg[b].reshape(512, 128).astype(f32) * LOG2E
        return 0

    lax.fori_loop(0, 16, widen, 0)

    def o_copy(s, d):
        to = turn(zh, d)
        return remote(os_.at[s, to], og.at[s, zh], pair_of(o_zh, s, d - 1), dev(zh=to))

    def attend(s):
        for d in (1, 2, 3):
            source = turn(zh, -d)
            remote(qs.at[s, 0], qg.at[s, source], pair_of(q_zh, s, d - 1), dev(zh=source)).wait_recv()
        for d in (1, 2, 3):
            source = turn(y, -d)
            slot = kvg.at[s, source]
            remote(slot, slot, pair_of(k_y, s, d - 1), dev(y=source)).wait_recv()
        for b in range(16):
            columns = slice(b * 128, (b + 1) * 128)
            block = kvg[s, b % 4, b // 4]
            kaug[0:HW, columns] = block[0:HW]
            kaug[HW : 2 * HW, columns] = block[0:HW]
            vaug[0:HW, columns] = block[HW : 2 * HW]
        kaug[96:112] = mb[s]
        for b in range(4):
            scaled = qg[s, b].astype(f32) * (LOG2E / math.sqrt(HW))
            high = scaled.astype(bf16).astype(f32)
            stacked = jnp.concatenate(
                [high, scaled - high, jnp.where(iota((32, 128), 0) == 0, 1.0, 0.0)], axis=0
            )
            qaug[b * 128 : (b + 1) * 128] = stacked.T.astype(bf16)

        def block_rows(r, _):
            rows = pl.ds(pl.multiple_of(r * 256, 256), 256)
            scores = jnp.dot(qaug[rows], kaug[...], preferred_element_type=f32) + bf[rows]
            highest = jnp.max(scores, axis=1, keepdims=True)
            probs = jnp.exp2(scores - highest).astype(bf16)
            mixed = lax.dot_general(probs, vaug[...], NT, preferred_element_type=f32).T
            attended = (mixed[0:HW] / mixed[HW : HW + 1]).astype(bf16)
            os_[s, 2 * r] = attended[:, 0:128]
            os_[s, 2 * r + 1] = attended[:, 128:256]
            return 0

        lax.fori_loop(0, 2, block_rows, 0)
        for d in (1, 2, 3):
            o_copy(s, d).start()
        og[s, zh] = os_[s, zh]

    def attention(s, _):
        forward(s + 1)
        attend(s)
        return 0

    lax.fori_loop(0, S - 1, attention, 0)
    attend(S - 1)

    for zl_from in range(4):
        for d in (1, 2, 3):
            slot = wog.at[turn(x, -d) * 4 + zl_from]
            remote(slot, slot, pair_of(wo_x, d - 1, zl_from), dev(x=turn(x, -d))).wait_recv()
    wop[...] = jnp.zeros_like(wop)
    for half in range(2):
        blocks = wog[8 * half : 8 * half + 8].astype(f32)
        for side in range(2):
            wop[half, 0:HALF, side * F : (side + 1) * F] = (
                blocks[:, side * 24 : (side + 1) * 24].reshape(HALF, F).astype(bf16)
            )

    def a_copy(s):
        return remote(xs.at[s], at.at[core, s], pair_of(a_c, s), dev(core=other))

    def collect(s, _):
        for d in (1, 2, 3):
            source = turn(zh, -d)
            remote(os_.at[s, 0], og.at[s, source], pair_of(o_zh, s, d - 1), dev(zh=source)).wait_recv()
        stacked = jnp.concatenate([og[s].astype(f32).reshape(HALF, 128), jnp.zeros((64, 128), f32)], axis=0)
        tokens = stacked.T.astype(bf16)
        first, second = tokens[0:T], tokens[T : 2 * T]
        xs[s] = jnp.where(core == 0, second.astype(f32), first.astype(f32)).astype(bf16)
        a_copy(s).start()
        at[core, s] = jnp.where(core == 0, first.astype(f32), second.astype(f32)).astype(bf16)
        return 0

    lax.fori_loop(0, S, collect, 0)
    loads[4].wait()

    def finish(s, _):
        slot = at.at[other, s]
        remote(xs.at[s], slot, pair_of(a_c, s), dev(core=other)).wait_recv()
        projected = jnp.dot(at[0, s], wop[0], preferred_element_type=f32) + jnp.dot(
            at[1, s], wop[1], preferred_element_type=f32
        )
        opened = jax.nn.sigmoid(gate[s].astype(f32))
        out_ref[s] = (act[s].astype(f32) + opened * projected).astype(bf16)
        return 0

    lax.fori_loop(0, S, finish, 0)

    mask_core.wait_send()
    bias_core.wait_send()
    shifted_core.wait_send()
    for copy in (
        w_zl_copies + w_x_copies + wo_zl_copies + wo_x_copies + b_zh_copies + b_zl_copies + b_x_copies
        + m_zh_copies + m_y_copies
    ):
        copy.wait_send()

    def drain(s, _):
        for d in (1, 2, 3):
            kv_copy(s, d).wait_send()
            q_copy(s, d).wait_send()
            ky_copy(s, d).wait_send()
            o_copy(s, d).wait_send()
        a_copy(s).wait_send()
        return 0

    lax.fori_loop(0, S, drain, 0)


def body(
    activations, cond_scale, cond_shift, output_gate, pair_repr, bias_weight, query_weight, query_bias, key_weight,
    value_weight, output_weight, token_mask,
):
    vmem = pl.BlockSpec(memory_space=pltpu.VMEM)
    any_ = pl.BlockSpec(memory_space=pl.ANY)
    dma = pltpu.SemaphoreType.DMA
    scratch = [
        *[pltpu.VMEM((S, T, D), bf16)] * 4,
        pltpu.VMEM((T, 128, 128), bf16),
        dma((5,)),
        pltpu.VMEM((16, HW, WC), bf16),
        pltpu.VMEM((16, HW, F), bf16),
        pltpu.VMEM((2, 256, D), bf16),
        pltpu.VMEM((16, WC), f32),
        pltpu.VMEM((S, 2 * T, D), bf16),
        pltpu.VMEM((S, 4, 2 * HW, 128), bf16),
        pltpu.VMEM((S, 4, 4, 2 * HW, 128), bf16),
        pltpu.VMEM((S, 4, HW, 128), bf16),
        pltpu.VMEM((S, 4, HW, 128), bf16),
        pltpu.VMEM((8, T, 128), f32),
        pltpu.VMEM((2, 4, T, 128), bf16),
        pltpu.VMEM((4, 2 * T, 128), bf16),
        pltpu.VMEM((16, 4, 128, 128), bf16),
        pltpu.VMEM((512, KEYS), f32),
        pltpu.VMEM((16, 128), f32),
        pltpu.VMEM((16, 128), bf16),
        pltpu.VMEM((16, 128), bf16),
        pltpu.VMEM((4, 4, 16, 128), bf16),
        pltpu.VMEM((S, 16, KEYS), bf16),
        pltpu.VMEM((128, KEYS), bf16),
        pltpu.VMEM((128, KEYS), bf16),
        pltpu.VMEM((512, 128), bf16),
        pltpu.VMEM((S, 4, HW, 128), bf16),
        pltpu.VMEM((S, 4, HW, 128), bf16),
        pltpu.VMEM((S, T, 256), bf16),
        pltpu.VMEM((2, S, T, 256), bf16),
        dma((2, 3)),
        dma((2, 3, 4)),
        dma((2, 3)),
        dma((2, 3, 4)),
        dma((2, 3)),
        dma((2, 3)),
        dma((2, 3)),
        dma((2, 3, 4)),
        dma((2, 3)),
        dma((2, 3)),
        dma((2, S, 3)),
        dma((2, S, 3)),
        dma((2, S, 3)),
        dma((2, S, 3)),
        dma((2, S)),
    ]
    return pl.pallas_call(
        kernel,
        out_shape=jax.ShapeDtypeStruct((S, T, D), bf16),
        in_specs=[any_] * 5 + [vmem] * 7,
        out_specs=vmem,
        scratch_shapes=scratch,
        compiler_params=pltpu.CompilerParams(
            collective_id=0, has_side_effects=True, vmem_limit_bytes=56 * 2**20
        ),
        cost_estimate=pl.CostEstimate(flops=2 * 10**9, bytes_accessed=5 * 10**6, transcendentals=4 * 10**6),
        name="pair_attention",
    )(
        activations, cond_scale, cond_shift, output_gate, pair_repr, bias_weight, query_weight,
        query_bias.reshape(1, F), key_weight, value_weight, output_weight, token_mask,
    )


def solution(mesh):
    return jax.shard_map(
        body,
        mesh=mesh,
        in_specs=(
            P("noise", "row", None),
            P("noise", "row", None),
            P("noise", "row", None),
            P("noise", "row", None),
            P("row", "noise", None),
            P(),
            P("noise", None),
            P(),
            P("noise", None),
            P("noise", None),
            P("noise", None),
            P("noise", "row"),
        ),
        out_specs=P("noise", "row", None),
        check_vma=False,
    )
```

time: 391 us -> 120 us (0.31)
  the two profiles are of different devices: /device:TPU:1 before, /device:TPU:65 now
where the time goes in v1:
time: 120 us
  Pallas kernels  116 us (97%)
  local copies, waits for them, and re-layouts  4.42 us (4%)
    pallas_call x1, Pallas kernels, body(): pl.pallas_call(kernel, out_shape=jax.ShapeDtypeStruct((S, T, D), bf16), i...  116 us
    unnamed x2, local copies, waits for them, and re-layouts  3.16 us

profile of v1, /device:TPU:65, one launch (start us, length us, event | category | flops | bytes accessed | tf_op | source)
XLA Modules:
  0.0 120.0 jit_solution(9751007493150216529)
XLA Ops:
  0.0 1.3 %reshape.3.qb_ref = bf16[1,384]{1,0:T(2,128)(2,1)} reshape(bf16[384]{0:T(512)(128)(2,1)} %param.19) | data formatting | bytes 1536 | tf_op jit(solution)/shard_map/reshape | solution.py:484
  1.3 1.4 %copy.13.wb_ref = bf16[128,8]{1,0:T(8,128)(2,1)} copy(bf16[128,8]{0,1:T(8,128)(2,1)} %param.17) | data formatting | bytes 4096 | tf_op args[5]
  2.7 115.6 %pair_attention.1 = bf16[4,64,768]{2,1,0:T(8,128)(2,1)} custom-call(bf16[4,64,768]{2,1,0:T(8,128)(2,1)} %act_h.1, bf16[4,64,768]{2,1,0:T(8,128)(2,1)} %scale_h.1, bf16[4,64,768]{2,1,0:T(8,128)(2,1)} %shift_h.1, bf16[4,64,768]{2,1,0:T(8,128)(2,1)} %gate_h.1, bf16[64,128,128]{2,1,0:T(8,128)(2,1)} %pair_h.1, bf16[128,8]{1,0:T(8,128)(2,1)} %copy.13.wb_ref, ...), custom_call_target="tpu_custom_call" | custom-call | flops 2000000000 | bytes 5000000 | tf_op jit(solution)/shard_map/pair_attention/pallas_call | solution.py:471
  118.3 1.8 %copy.15 = bf16[4,64,768]{2,1,0:T(8,128)(2,1)} copy(bf16[4,64,768]{2,1,0:T(8,128)(2,1)} %pair_attention.1) | data formatting | bytes 786432

commit v2 on v1

--- a/solution.py
+++ b/solution.py
@@ -68,6 +68,48 @@
     def pair_of(sem, *index):
         return sem.at[(0, *index)], sem.at[(1, *index)]
 
+    def hop(buffer, sems, way, origin):
+        slot = buffer.at[x * 4 + origin]
+        return remote(slot, slot, pair_of(sems, way, origin), dev(zl=turn(zl, 1 if way == 0 else -1)))
+
+    def to_x(buffer, sems, origin, d):
+        slot = buffer.at[x * 4 + origin]
+        return remote(slot, slot, pair_of(sems, d - 1, origin), dev(x=turn(x, d)))
+
+    def pass_on(buffer, z_sems, x_sems, origin, ways):
+        for way in ways:
+
+            @pl.when(zl < 3 if way == 0 else zl > 0)
+            def _():
+                hop(buffer, z_sems, way, origin).start()
+
+        for d in (1, 2, 3):
+            to_x(buffer, x_sems, origin, d).start()
+
+    def line_step(buffer, z_sems, x_sems, k):
+        @pl.when(zl >= k)
+        def _():
+            hop(buffer, z_sems, 0, zl - k).wait_recv()
+            pass_on(buffer, z_sems, x_sems, zl - k, (0,))
+
+        @pl.when(zl + k <= 3)
+        def _():
+            hop(buffer, z_sems, 1, zl + k).wait_recv()
+            pass_on(buffer, z_sems, x_sems, zl + k, (1,))
+
+    def line_drain(buffer, z_sems, x_sems):
+        for origin in range(4):
+            for d in (1, 2, 3):
+                to_x(buffer, x_sems, origin, d).wait_send()
+
+            @pl.when((zl < 3) & (zl >= origin))
+            def _():
+                hop(buffer, z_sems, 0, origin).wait_send()
+
+            @pl.when((zl > 0) & (zl <= origin))
+            def _():
+                hop(buffer, z_sems, 1, origin).wait_send()
+
     barrier = pltpu.get_barrier_semaphore()
     for d in (1, 2, 3):
         for where in (dev(zh=turn(zh, d)), dev(zl=turn(zl, d)), dev(x=turn(x, d)), dev(y=turn(y, d))):
@@ -83,37 +125,7 @@
     for load in loads:
         load.start()
 
-    def chosen(first):
-        return ((iota((F, WC), 0) == iota((F, WC), 1) - first + HALF * core)
-                & (iota((F, WC), 1) >= first) & (iota((F, WC), 1) < first + HALF)).astype(f32).astype(bf16)
-
-    weights = (
-        jnp.dot(wk_ref[...], chosen(0), preferred_element_type=f32)
-        + jnp.dot(wv_ref[...], chosen(HALF), preferred_element_type=f32)
-        + jnp.dot(wq_ref[...], chosen(2 * HALF), preferred_element_type=f32)
-    )
-    qrow[...] = jnp.dot(
-        jnp.broadcast_to(qb_ref[...].astype(f32), (16, F)).astype(bf16), chosen(2 * HALF), preferred_element_type=f32
-    )
-    wg[noise] = weights.astype(bf16)
-    wo = wo_ref[...].astype(f32)
-    wog[noise] = jnp.concatenate([wo[:, :F], wo[:, F:]], axis=0).astype(bf16)
-    lanes = (iota((T, 128), 1) == iota((T, 128), 0) + T * core).astype(f32).astype(bf16)
-    mk[...] = jnp.zeros_like(mk)
-    mk[0:S] = jnp.dot(mask_ref[...].astype(f32).astype(bf16), lanes, preferred_element_type=f32)
-    mks[...] = mk[...].astype(bf16)
-
-    pl.semaphore_wait(barrier, 13)
-
-    w_zl_copies = [
-        remote(wg.at[noise], wg.at[noise], pair_of(w_zl, d - 1), dev(zl=turn(zl, d))) for d in (1, 2, 3)
-    ]
-    for copy in w_zl_copies:
-        copy.start()
-    mask_core = remote(mks, mko, pair_of(c_sem, 0), dev(core=other))
-    mask_core.start()
-
-    wb = jnp.concatenate([wb_ref[...].astype(f32), jnp.zeros((128, 120), f32)], axis=1)
+    wb = jnp.concatenate([wb_ref[...].astype(f32), jnp.zeros((120, 128), f32)], axis=0).T
     wsum = jnp.sum(wb, axis=0, keepdims=True)
     wide = jnp.concatenate([wb, jnp.full((128, 128), 1.0 / 128, f32)], axis=1).astype(bf16)
     mean_at = jnp.where(iota((128, 128), 1) == 8, 1.0 / 128, 0.0).astype(bf16)
@@ -134,37 +146,36 @@
 
     lax.fori_loop(0, 8, pair_rows, 0)
     btb[...] = bt[...].astype(bf16).reshape(2, 4, T, 128)
+
+    def chosen(first):
+        return ((iota((F, WC), 0) == iota((F, WC), 1) - first + HALF * core)
+                & (iota((F, WC), 1) >= first) & (iota((F, WC), 1) < first + HALF)).astype(f32).astype(bf16)
+
+    weights = (
+        jnp.dot(wk_ref[...], chosen(0), preferred_element_type=f32)
+        + jnp.dot(wv_ref[...], chosen(HALF), preferred_element_type=f32)
+        + jnp.dot(wq_ref[...], chosen(2 * HALF), preferred_element_type=f32)
+    )
+    qrow[...] = jnp.dot(
+        jnp.broadcast_to(qb_ref[...].astype(f32).reshape(1, F), (16, F)).astype(bf16), chosen(2 * HALF), preferred_element_type=f32
+    )
+    wg[noise] = weights.astype(bf16)
+    wo = wo_ref[...].astype(f32)
+    wog[noise] = jnp.concatenate([wo[:, :F], wo[:, F:]], axis=0).astype(bf16)
+    lanes = (iota((T, 128), 1) == iota((T, 128), 0) + T * core).astype(f32).astype(bf16)
+    mk[...] = jnp.zeros_like(mk)
+    mk[0:S] = jnp.dot(mask_ref[...].astype(f32).astype(bf16), lanes, preferred_element_type=f32)
+    mks[...] = mk[...].astype(bf16)
+
+    pl.semaphore_wait(barrier, 13)
+
     here = pl.ds(pl.multiple_of(core * T, T), T)
     bias_core = remote(btb.at[other], bc.at[:, here], pair_of(c_sem, 1), dev(core=other))
     bias_core.start()
     bc[:, here] = btb[core]
-
-    for load in loads[1:4]:
-        load.wait()
-
-    def norm_rows(s, _):
-        normed = layer_norm(act[s].astype(f32))
-        sh[s, here] = (scale[s].astype(f32) * normed + shift[s].astype(f32)).astype(bf16)
-        return 0
-
-    lax.fori_loop(0, S, norm_rows, 0)
-    shifted_core = remote(sh.at[:, here], sh.at[:, here], pair_of(c_sem, 2), dev(core=other))
-    shifted_core.start()
-
-    def weights_x(zl_from):
-        block = x * 4 + zl_from
-        copies = []
-        for d in (1, 2, 3):
-            copies.append(remote(wg.at[block], wg.at[block], pair_of(w_x, d - 1, zl_from), dev(x=turn(x, d))))
-            copies[-1].start()
-        return copies
-
-    w_x_copies = weights_x(zl)
-    for d in (1, 2, 3):
-        source = turn(zl, -d)
-        slot = wg.at[x * 4 + source]
-        remote(slot, slot, pair_of(w_zl, d - 1), dev(zl=source)).wait_recv()
-        w_x_copies += weights_x(source)
+    pass_on(wg, w_zl, w_x, zl, (0, 1))
+    mask_core = remote(mks, mko, pair_of(c_sem, 0), dev(core=other))
+    mask_core.start()
 
     there = pl.ds(pl.multiple_of(other * T, T), T)
     remote(btb.at[other], bc.at[:, there], pair_of(c_sem, 1), dev(core=other)).wait_recv()
@@ -174,44 +185,27 @@
         b_zh_copies.append(remote(bc.at[to], bg.at[noise, zh], pair_of(b_zh, d - 1), dev(zh=to)))
         b_zh_copies[-1].start()
     bg[noise, zh] = bc[zh]
+    for load in loads[1:4]:
+        load.wait()
+
+    def norm_rows(s, _):
+        normed = layer_norm(act[s].astype(f32))
+        sh[s, here] = (scale[s].astype(f32) * normed + shift[s].astype(f32)).astype(bf16)
+        return 0
+
+    lax.fori_loop(0, S, norm_rows, 0)
+    shifted_core = remote(sh.at[:, here], sh.at[:, here], pair_of(c_sem, 2), dev(core=other))
+    shifted_core.start()
+
+    for k in (1, 2, 3):
+        line_step(wg, w_zl, w_x, k)
+
     mask_core.wait_recv()
     mg[y, zh] = mks[...] + mko[...]
     m_zh_copies = []
     for d in (1, 2, 3):
         m_zh_copies.append(remote(mg.at[y, zh], mg.at[y, zh], pair_of(m_zh, d - 1), dev(zh=turn(zh, d))))
         m_zh_copies[-1].start()
-    wo_zl_copies = [
-        remote(wog.at[noise], wog.at[noise], pair_of(wo_zl, d - 1), dev(zl=turn(zl, d))) for d in (1, 2, 3)
-    ]
-    for copy in wo_zl_copies:
-        copy.start()
-
-    def bias_x(zl_from):
-        block = x * 4 + zl_from
-        copies = []
-        for d in (1, 2, 3):
-            copies.append(remote(bg.at[block], bg.at[block], pair_of(b_x, d - 1, zl_from), dev(x=turn(x, d))))
-            copies[-1].start()
-        return copies
-
-    for d in (1, 2, 3):
-        source = turn(zh, -d)
-        remote(bc.at[0], bg.at[noise, source], pair_of(b_zh, d - 1), dev(zh=source)).wait_recv()
-    b_zl_copies = [
-        remote(bg.at[noise], bg.at[noise], pair_of(b_zl, d - 1), dev(zl=turn(zl, d))) for d in (1, 2, 3)
-    ]
-    for copy in b_zl_copies:
-        copy.start()
-    b_x_copies = bias_x(zl)
-
-    for d in (1, 2, 3):
-        source = turn(zh, -d)
-        slot = mg.at[y, source]
-        remote(slot, slot, pair_of(m_zh, d - 1), dev(zh=source)).wait_recv()
-    m_y_copies = []
-    for d in (1, 2, 3):
-        m_y_copies.append(remote(mg.at[y], mg.at[y], pair_of(m_y, d - 1), dev(y=turn(y, d))))
-        m_y_copies[-1].start()
 
     remote(sh.at[:, there], sh.at[:, there], pair_of(c_sem, 2), dev(core=other)).wait_recv()
     for zl_from in range(4):
@@ -226,6 +220,17 @@
     def q_copy(s, d):
         to = turn(zh, d)
         return remote(qs.at[s, to], qg.at[s, zh], pair_of(q_zh, s, d - 1), dev(zh=to))
+
+    def ky_copy(s, d, e):
+        slot = kvg.at[s, y, turn(zh, -e)]
+        return remote(slot, slot, pair_of(k_y, s, d - 1, e), dev(y=turn(y, d)))
+
+    def forward(s):
+        for e in (1, 3, 2):
+            source = turn(zh, -e)
+            remote(kvs.at[s, 0], kvg.at[s, y, source], pair_of(k_zh, s, e - 1), dev(zh=source)).wait_recv()
+            for d in (1, 2, 3):
+                ky_copy(s, d, e).start()
 
     def project(s, _):
         rows = jnp.dot(sh[s], wg[...].reshape(D, WC), preferred_element_type=f32) + qrow[0:1]
@@ -234,15 +239,45 @@
             kvs[s, h, 0:HW] = flipped[h * HW : (h + 1) * HW]
             kvs[s, h, HW : 2 * HW] = flipped[HALF + h * HW : HALF + (h + 1) * HW]
             qs[s, h] = flipped[2 * HALF + h * HW : 2 * HALF + (h + 1) * HW]
-        for d in (1, 2, 3):
-            kv_copy(s, d).start()
-        for d in (1, 2, 3):
-            q_copy(s, d).start()
         kvg[s, y, zh] = kvs[s, zh]
         qg[s, zh] = qs[s, zh]
         return 0
 
-    lax.fori_loop(0, S, project, 0)
+    def exchange(s, _):
+        for d in (1, 2, 3):
+            kv_copy(s, d).start()
+        for d in (1, 2, 3):
+            q_copy(s, d).start()
+        for d in (1, 2, 3):
+            ky_copy(s, d, 0).start()
+        return 0
+
+    project(0, 0)
+    exchange(0, 0)
+
+    for d in (1, 2, 3):
+        source = turn(zh, -d)
+        remote(bc.at[0], bg.at[noise, source], pair_of(b_zh, d - 1), dev(zh=source)).wait_recv()
+    pass_on(bg, b_zl, b_x, zl, (0, 1))
+    lax.fori_loop(1, S, project, 0)
+    line_step(bg, b_zl, b_x, 1)
+    exchange(1, 0)
+    for k in (2, 3):
+        line_step(bg, b_zl, b_x, k)
+    wo_zl_copies = [
+        remote(wog.at[noise], wog.at[noise], pair_of(wo_zl, d - 1), dev(zl=turn(zl, d))) for d in (1, 2, 3)
+    ]
+    for copy in wo_zl_copies:
+        copy.start()
+    for d in (1, 2, 3):
+        source = turn(zh, -d)
+        slot = mg.at[y, source]
+        remote(slot, slot, pair_of(m_zh, d - 1), dev(zh=source)).wait_recv()
+    m_y_copies = []
+    for d in (1, 2, 3):
+        m_y_copies.append(remote(mg.at[y], mg.at[y], pair_of(m_y, d - 1), dev(y=turn(y, d))))
+        m_y_copies[-1].start()
+
 
     def wo_x_send(zl_from):
         block = x * 4 + zl_from
@@ -252,29 +287,14 @@
             copies[-1].start()
         return copies
 
-    for d in (1, 2, 3):
-        source = turn(zl, -d)
-        slot = bg.at[x * 4 + source]
-        remote(slot, slot, pair_of(b_zl, d - 1), dev(zl=source)).wait_recv()
-        b_x_copies += bias_x(source)
+    forward(0)
+    exchange(2, 0)
     wo_x_copies = wo_x_send(zl)
     for d in (1, 2, 3):
         source = turn(zl, -d)
         slot = wog.at[x * 4 + source]
         remote(slot, slot, pair_of(wo_zl, d - 1), dev(zl=source)).wait_recv()
         wo_x_copies += wo_x_send(source)
-
-    def ky_copy(s, d):
-        return remote(kvg.at[s, y], kvg.at[s, y], pair_of(k_y, s, d - 1), dev(y=turn(y, d)))
-
-    def forward(s):
-        for d in (1, 2, 3):
-            source = turn(zh, -d)
-            remote(kvs.at[s, 0], kvg.at[s, y, source], pair_of(k_zh, s, d - 1), dev(zh=source)).wait_recv()
-        for d in (1, 2, 3):
-            ky_copy(s, d).start()
-
-    forward(0)
 
     for d in (1, 2, 3):
         source = turn(y, -d)
@@ -289,6 +309,9 @@
     kaug[112:128] = jnp.zeros((16, KEYS), bf16)
     vaug[HW:128] = jnp.where(iota((80, KEYS), 0) == 0, 1.0, 0.0).astype(bf16)
 
+    forward(1)
+    exchange(3, 0)
+
     for zl_from in range(4):
         for d in (1, 2, 3):
             slot = bg.at[turn(x, -d) * 4 + zl_from]
@@ -311,8 +334,9 @@
             remote(qs.at[s, 0], qg.at[s, source], pair_of(q_zh, s, d - 1), dev(zh=source)).wait_recv()
         for d in (1, 2, 3):
             source = turn(y, -d)
-            slot = kvg.at[s, source]
-            remote(slot, slot, pair_of(k_y, s, d - 1), dev(y=source)).wait_recv()
+            for e in range(4):
+                slot = kvg.at[s, source, turn(zh, -e)]
+                remote(slot, slot, pair_of(k_y, s, d - 1, e), dev(y=source)).wait_recv()
         for b in range(16):
             columns = slice(b * 128, (b + 1) * 128)
             block = kvg[s, b % 4, b // 4]
@@ -345,12 +369,15 @@
         og[s, zh] = os_[s, zh]
 
     def attention(s, _):
-        forward(s + 1)
         attend(s)
-        return 0
-
-    lax.fori_loop(0, S - 1, attention, 0)
-    attend(S - 1)
+
+        @pl.when(s < 2)
+        def _():
+            forward(s + 2)
+
+        return 0
+
+    lax.fori_loop(0, S, attention, 0)
 
     for zl_from in range(4):
         for d in (1, 2, 3):
@@ -397,17 +424,18 @@
     mask_core.wait_send()
     bias_core.wait_send()
     shifted_core.wait_send()
-    for copy in (
-        w_zl_copies + w_x_copies + wo_zl_copies + wo_x_copies + b_zh_copies + b_zl_copies + b_x_copies
-        + m_zh_copies + m_y_copies
-    ):
+    for copy in (wo_zl_copies + wo_x_copies + b_zh_copies + m_zh_copies + m_y_copies):
         copy.wait_send()
+
+    line_drain(wg, w_zl, w_x)
+    line_drain(bg, b_zl, b_x)
 
     def drain(s, _):
         for d in (1, 2, 3):
             kv_copy(s, d).wait_send()
             q_copy(s, d).wait_send()
-            ky_copy(s, d).wait_send()
+            for e in range(4):
+                ky_copy(s, d, e).wait_send()
             o_copy(s, d).wait_send()
         a_copy(s).wait_send()
         return 0
@@ -452,19 +480,19 @@
         pltpu.VMEM((S, 4, HW, 128), bf16),
         pltpu.VMEM((S, T, 256), bf16),
         pltpu.VMEM((2, S, T, 256), bf16),
-        dma((2, 3)),
+        dma((2, 2, 4)),
         dma((2, 3, 4)),
         dma((2, 3)),
         dma((2, 3, 4)),
         dma((2, 3)),
         dma((2, 3)),
-        dma((2, 3)),
+        dma((2, 2, 4)),
         dma((2, 3, 4)),
         dma((2, 3)),
         dma((2, 3)),
         dma((2, S, 3)),
         dma((2, S, 3)),
-        dma((2, S, 3)),
+        dma((2, S, 3, 4)),
         dma((2, S, 3)),
         dma((2, S)),
     ]
@@ -480,8 +508,8 @@
         cost_estimate=pl.CostEstimate(flops=2 * 10**9, bytes_accessed=5 * 10**6, transcendentals=4 * 10**6),
         name="pair_attention",
     )(
-        activations, cond_scale, cond_shift, output_gate, pair_repr, bias_weight, query_weight,
-        query_bias.reshape(1, F), key_weight, value_weight, output_weight, token_mask,
+        activations, cond_scale, cond_shift, output_gate, pair_repr, bias_weight.T, query_weight,
+        query_bias, key_weight, value_weight, output_weight, token_mask,
     )
 
 

time: 120 us -> 102 us (0.85)
  the two profiles are of different devices: /device:TPU:65 before, /device:TPU:1 now
where the time goes in v2:
time: 102 us; the launch traced here: 99.9 us
  Pallas kernels  98.1 us (96%)
  local copies, waits for them, and re-layouts  1.77 us (2%)
    pallas_call x1, Pallas kernels, body(): pl.pallas_call(kernel, out_shape=jax.ShapeDtypeStruct((S, T, D), bf16), i...  98.1 us

profile of v2, /device:TPU:1, one launch (start us, length us, event | category | flops | bytes accessed | tf_op | source)
XLA Modules:
  0.0 99.9 jit_solution(1970596338996378523)
XLA Ops:
  0.0 98.1 %pair_attention.1 = bf16[4,64,768]{2,1,0:T(8,128)(2,1)} custom-call(bf16[4,64,768]{2,1,0:T(8,128)(2,1)} %act_h.1, bf16[4,64,768]{2,1,0:T(8,128)(2,1)} %scale_h.1, bf16[4,64,768]{2,1,0:T(8,128)(2,1)} %shift_h.1, bf16[4,64,768]{2,1,0:T(8,128)(2,1)} %gate_h.1, bf16[64,128,128]{2,1,0:T(8,128)(2,1)} %pair_h.1, bf16[8,128]{1,0:T(8,128)(2,1)} %bitcast.1, ...), custom_call_target="tpu_custom_call" | custom-call | flops 2000000000 | bytes 5000000 | tf_op jit(solution)/shard_map/pair_attention/pallas_call | solution.py:499
  98.2 1.8 %copy.14 = bf16[4,64,768]{2,1,0:T(8,128)(2,1)} copy(bf16[4,64,768]{2,1,0:T(8,128)(2,1)} %pair_attention.1) | data formatting | bytes 786432

commit v3 on v2

--- a/solution.py
+++ b/solution.py
@@ -38,9 +38,9 @@
 
 
 def kernel(
-    act_h, scale_h, shift_h, gate_h, pair_h, wb_ref, wq_ref, qb_ref, wk_ref, wv_ref, wo_ref, mask_ref,
-    out_ref,
-    act, scale, shift, gate, pair, local_sem,
+    act_h, scale_h, shift_h, gate_h, pair_h, wb_h, wq_h, qb_ref, wk_h, wv_h, wo_h, mask_h,
+    out_h,
+    act, scale, shift, gate, pair, wb_ref, wq_ref, wk_ref, wv_ref, wo_ref, mask_ref, out, local_sem, out_sem,
     wg, wog, wop, qrow,
     sh, kvs, kvg, qs, qg,
     bt, btb, bc, bg, bf,
@@ -119,33 +119,17 @@
     loads = [
         pltpu.make_async_copy(source, target, local_sem.at[i])
         for i, (source, target) in enumerate(
-            ((pair_h, pair), (act_h, act), (scale_h, scale), (shift_h, shift), (gate_h, gate))
+            (
+                (pair_h, pair), (wb_h, wb_ref), (wq_h, wq_ref), (wk_h, wk_ref), (wv_h, wv_ref), (wo_h, wo_ref),
+                (mask_h, mask_ref), (act_h, act), (scale_h, scale), (shift_h, shift), (gate_h, gate),
+            )
         )
     ]
     for load in loads:
         load.start()
 
-    wb = jnp.concatenate([wb_ref[...].astype(f32), jnp.zeros((120, 128), f32)], axis=0).T
-    wsum = jnp.sum(wb, axis=0, keepdims=True)
-    wide = jnp.concatenate([wb, jnp.full((128, 128), 1.0 / 128, f32)], axis=1).astype(bf16)
-    mean_at = jnp.where(iota((128, 128), 1) == 8, 1.0 / 128, 0.0).astype(bf16)
-    loads[0].wait()
-
-    def pair_rows(step, _):
-        tile = pair[pl.ds(step * 8, 8)].reshape(1024, 128)
-        both = jnp.dot(tile, wide, preferred_element_type=f32)
-        mean = both[:, 128:]
-        centred = tile.astype(f32) - mean
-        square = (centred * centred).astype(bf16)
-        table = both[:, :128] - mean * wsum + jnp.dot(square, mean_at, preferred_element_type=f32)
-        for i in range(8):
-            flipped = table[i * 128 : (i + 1) * 128].T
-            bias = flipped[0:8] * lax.rsqrt(flipped[8:9] + epsilon)
-            bt[:, pl.ds(step * 8 + i, 1), :] = bias.reshape(8, 1, 128)
-        return 0
-
-    lax.fori_loop(0, 8, pair_rows, 0)
-    btb[...] = bt[...].astype(bf16).reshape(2, 4, T, 128)
+    for load in loads[2:7]:
+        load.wait()
 
     def chosen(first):
         return ((iota((F, WC), 0) == iota((F, WC), 1) - first + HALF * core)
@@ -167,15 +151,43 @@
     mk[0:S] = jnp.dot(mask_ref[...].astype(f32).astype(bf16), lanes, preferred_element_type=f32)
     mks[...] = mk[...].astype(bf16)
 
+    loads[1].wait()
+    wb = jnp.concatenate([wb_ref[...].astype(f32), jnp.zeros((120, 128), f32)], axis=0).T
+    wsum = jnp.sum(wb, axis=0, keepdims=True)
+    wide = jnp.concatenate([wb, jnp.full((128, 128), 1.0 / 128, f32)], axis=1).astype(bf16)
+    mean_at = jnp.where(iota((128, 128), 1) == 8, 1.0 / 128, 0.0).astype(bf16)
+    loads[0].wait()
+
+    def pair_rows(step, _):
+        tile = pair[pl.ds(step * 8, 8)].reshape(1024, 128)
+        both = jnp.dot(tile, wide, preferred_element_type=f32)
+        mean = both[:, 128:]
+        centred = tile.astype(f32) - mean
+        square = (centred * centred).astype(bf16)
+        table = both[:, :128] - mean * wsum + jnp.dot(square, mean_at, preferred_element_type=f32)
+        for i in range(8):
+            flipped = table[i * 128 : (i + 1) * 128].T
+            bias = flipped[0:8] * lax.rsqrt(flipped[8:9] + epsilon)
+            bt[:, pl.ds(step * 8 + i, 1), :] = bias.reshape(8, 1, 128)
+        return 0
+
+    lax.fori_loop(0, 4, pair_rows, 0)
+
     pl.semaphore_wait(barrier, 13)
 
+    pass_on(wg, w_zl, w_x, zl, (0, 1))
+    mask_core = remote(mks, mko, pair_of(c_sem, 0), dev(core=other))
+    mask_core.start()
+
+    lax.fori_loop(4, 6, pair_rows, 0)
+    line_step(wg, w_zl, w_x, 1)
+    lax.fori_loop(6, 8, pair_rows, 0)
+    btb[...] = bt[...].astype(bf16).reshape(2, 4, T, 128)
     here = pl.ds(pl.multiple_of(core * T, T), T)
     bias_core = remote(btb.at[other], bc.at[:, here], pair_of(c_sem, 1), dev(core=other))
     bias_core.start()
     bc[:, here] = btb[core]
-    pass_on(wg, w_zl, w_x, zl, (0, 1))
-    mask_core = remote(mks, mko, pair_of(c_sem, 0), dev(core=other))
-    mask_core.start()
+    line_step(wg, w_zl, w_x, 2)
 
     there = pl.ds(pl.multiple_of(other * T, T), T)
     remote(btb.at[other], bc.at[:, there], pair_of(c_sem, 1), dev(core=other)).wait_recv()
@@ -185,7 +197,8 @@
         b_zh_copies.append(remote(bc.at[to], bg.at[noise, zh], pair_of(b_zh, d - 1), dev(zh=to)))
         b_zh_copies[-1].start()
     bg[noise, zh] = bc[zh]
-    for load in loads[1:4]:
+    line_step(wg, w_zl, w_x, 3)
+    for load in loads[7:10]:
         load.wait()
 
     def norm_rows(s, _):
@@ -196,9 +209,6 @@
     lax.fori_loop(0, S, norm_rows, 0)
     shifted_core = remote(sh.at[:, here], sh.at[:, here], pair_of(c_sem, 2), dev(core=other))
     shifted_core.start()
-
-    for k in (1, 2, 3):
-        line_step(wg, w_zl, w_x, k)
 
     mask_core.wait_recv()
     mg[y, zh] = mks[...] + mko[...]
@@ -406,9 +416,6 @@
         at[core, s] = jnp.where(core == 0, first.astype(f32), second.astype(f32)).astype(bf16)
         return 0
 
-    lax.fori_loop(0, S, collect, 0)
-    loads[4].wait()
-
     def finish(s, _):
         slot = at.at[other, s]
         remote(xs.at[s], slot, pair_of(a_c, s), dev(core=other)).wait_recv()
@@ -416,10 +423,20 @@
             at[1, s], wop[1], preferred_element_type=f32
         )
         opened = jax.nn.sigmoid(gate[s].astype(f32))
-        out_ref[s] = (act[s].astype(f32) + opened * projected).astype(bf16)
-        return 0
-
-    lax.fori_loop(0, S, finish, 0)
+        out[s] = (act[s].astype(f32) + opened * projected).astype(bf16)
+        pltpu.make_async_copy(out.at[s], out_h.at[s], out_sem.at[s]).start()
+        return 0
+
+    loads[10].wait()
+    collect(0, 0)
+
+    def last(s, _):
+        collect(s + 1, 0)
+        finish(s, 0)
+        return 0
+
+    lax.fori_loop(0, S - 1, last, 0)
+    finish(S - 1, 0)
 
     mask_core.wait_send()
     bias_core.wait_send()
@@ -438,6 +455,7 @@
                 ky_copy(s, d, e).wait_send()
             o_copy(s, d).wait_send()
         a_copy(s).wait_send()
+        pltpu.make_async_copy(out.at[s], out_h.at[s], out_sem.at[s]).wait()
         return 0
 
     lax.fori_loop(0, S, drain, 0)
@@ -453,7 +471,13 @@
     scratch = [
         *[pltpu.VMEM((S, T, D), bf16)] * 4,
         pltpu.VMEM((T, 128, 128), bf16),
-        dma((5,)),
+        pltpu.VMEM((8, 128), bf16),
+        *[pltpu.VMEM((HW, F), bf16)] * 3,
+        pltpu.VMEM((F // 16, D), bf16),
+        pltpu.VMEM((S, T), jnp.int32),
+        pltpu.VMEM((S, T, D), bf16),
+        dma((11,)),
+        dma((S,)),
         pltpu.VMEM((16, HW, WC), bf16),
         pltpu.VMEM((16, HW, F), bf16),
         pltpu.VMEM((2, 256, D), bf16),
@@ -499,8 +523,8 @@
     return pl.pallas_call(
         kernel,
         out_shape=jax.ShapeDtypeStruct((S, T, D), bf16),
-        in_specs=[any_] * 5 + [vmem] * 7,
-        out_specs=vmem,
+        in_specs=[any_] * 7 + [vmem] + [any_] * 4,
+        out_specs=any_,
         scratch_shapes=scratch,
         compiler_params=pltpu.CompilerParams(
             collective_id=0, has_side_effects=True, vmem_limit_bytes=56 * 2**20

time: 102 us -> 97.6 us (0.957); the launches traced: 99.9 us -> 97.5 us
  Pallas kernels: 98.1 us -> 95.7 us
    pallas_call x1, Pallas kernels: 98.1 us -> 95.7 us  [body(): pl.pallas_call(kernel, out_shape=jax.ShapeDtypeStruct((S, T, D), bf16), i...]
where the time goes in v3:
time: 97.6 us; the launch traced here: 97.5 us
  Pallas kernels  95.7 us (98%)
  local copies, waits for them, and re-layouts  1.77 us (2%)
    pallas_call x1, Pallas kernels, body(): pl.pallas_call(kernel, out_shape=jax.ShapeDtypeStruct((S, T, D), bf16), i...  95.7 us

profile of v3, /device:TPU:1, one launch (start us, length us, event | category | flops | bytes accessed | tf_op | source)
XLA Modules:
  0.0 97.5 jit_solution(5113818350726458747)
XLA Ops:
  0.0 95.7 %pair_attention.1 = bf16[4,64,768]{2,1,0:T(8,128)(2,1)} custom-call(bf16[4,64,768]{2,1,0:T(8,128)(2,1)} %act_h.1, bf16[4,64,768]{2,1,0:T(8,128)(2,1)} %scale_h.1, bf16[4,64,768]{2,1,0:T(8,128)(2,1)} %shift_h.1, bf16[4,64,768]{2,1,0:T(8,128)(2,1)} %gate_h.1, bf16[64,128,128]{2,1,0:T(8,128)(2,1)} %pair_h.1, bf16[8,128]{1,0:T(8,128)(2,1)} %bitcast.1, ...), custom_call_target="tpu_custom_call" | custom-call | flops 2000000000 | bytes 5000000 | tf_op jit(solution)/shard_map/pair_attention/pallas_call | solution.py:523
  95.7 1.8 %copy.14 = bf16[4,64,768]{2,1,0:T(8,128)(2,1)} copy(bf16[4,64,768]{2,1,0:T(8,128)(2,1)} %pair_attention.1) | data formatting | bytes 786432

commit v4 on v3

--- a/solution.py
+++ b/solution.py
@@ -257,10 +257,12 @@
         for d in (1, 2, 3):
             kv_copy(s, d).start()
         for d in (1, 2, 3):
+            ky_copy(s, d, 0).start()
+        return 0
+
+    def exchange_q(s):
+        for d in (1, 2, 3):
             q_copy(s, d).start()
-        for d in (1, 2, 3):
-            ky_copy(s, d, 0).start()
-        return 0
 
     project(0, 0)
     exchange(0, 0)
@@ -272,6 +274,7 @@
     lax.fori_loop(1, S, project, 0)
     line_step(bg, b_zl, b_x, 1)
     exchange(1, 0)
+    exchange_q(0)
     for k in (2, 3):
         line_step(bg, b_zl, b_x, k)
     wo_zl_copies = [
@@ -299,6 +302,7 @@
 
     forward(0)
     exchange(2, 0)
+    exchange_q(1)
     wo_x_copies = wo_x_send(zl)
     for d in (1, 2, 3):
         source = turn(zl, -d)
@@ -321,6 +325,8 @@
 
     forward(1)
     exchange(3, 0)
+    exchange_q(2)
+    exchange_q(3)
 
     for zl_from in range(4):
         for d in (1, 2, 3):
@@ -363,17 +369,17 @@
             qaug[b * 128 : (b + 1) * 128] = stacked.T.astype(bf16)
 
         def block_rows(r, _):
-            rows = pl.ds(pl.multiple_of(r * 256, 256), 256)
+            rows = slice(0, 512)
             scores = jnp.dot(qaug[rows], kaug[...], preferred_element_type=f32) + bf[rows]
             highest = jnp.max(scores, axis=1, keepdims=True)
             probs = jnp.exp2(scores - highest).astype(bf16)
             mixed = lax.dot_general(probs, vaug[...], NT, preferred_element_type=f32).T
             attended = (mixed[0:HW] / mixed[HW : HW + 1]).astype(bf16)
-            os_[s, 2 * r] = attended[:, 0:128]
-            os_[s, 2 * r + 1] = attended[:, 128:256]
+            for b in range(4):
+                os_[s, b] = attended[:, b * 128 : (b + 1) * 128]
             return 0
 
-        lax.fori_loop(0, 2, block_rows, 0)
+        block_rows(0, 0)
         for d in (1, 2, 3):
             o_copy(s, d).start()
         og[s, zh] = os_[s, zh]

time: 97.6 us -> 95.7 us (0.981)
  Pallas kernels: 95.7 us -> 93.8 us
    pallas_call x1, Pallas kernels: 95.7 us -> 93.8 us  [body(): pl.pallas_call(kernel, out_shape=jax.ShapeDtypeStruct((S, T, D), bf16), i...]
where the time goes in v4:
time: 95.7 us; the launch traced here: 95.6 us
  Pallas kernels  93.8 us (98%)
  local copies, waits for them, and re-layouts  1.77 us (2%)
    pallas_call x1, Pallas kernels, body(): pl.pallas_call(kernel, out_shape=jax.ShapeDtypeStruct((S, T, D), bf16), i...  93.8 us

profile of v4, /device:TPU:1, one launch (start us, length us, event | category | flops | bytes accessed | tf_op | source)
XLA Modules:
  0.0 95.6 jit_solution(3262805722182996602)
XLA Ops:
  0.0 93.8 %pair_attention.1 = bf16[4,64,768]{2,1,0:T(8,128)(2,1)} custom-call(bf16[4,64,768]{2,1,0:T(8,128)(2,1)} %act_h.1, bf16[4,64,768]{2,1,0:T(8,128)(2,1)} %scale_h.1, bf16[4,64,768]{2,1,0:T(8,128)(2,1)} %shift_h.1, bf16[4,64,768]{2,1,0:T(8,128)(2,1)} %gate_h.1, bf16[64,128,128]{2,1,0:T(8,128)(2,1)} %pair_h.1, bf16[8,128]{1,0:T(8,128)(2,1)} %bitcast.1, ...), custom_call_target="tpu_custom_call" | custom-call | flops 2000000000 | bytes 5000000 | tf_op jit(solution)/shard_map/pair_attention/pallas_call | solution.py:529
  93.8 1.8 %copy.14 = bf16[4,64,768]{2,1,0:T(8,128)(2,1)} copy(bf16[4,64,768]{2,1,0:T(8,128)(2,1)} %pair_attention.1) | data formatting | bytes 786432

commit v5 on v4

--- a/solution.py
+++ b/solution.py
@@ -152,26 +152,25 @@
     mks[...] = mk[...].astype(bf16)
 
     loads[1].wait()
-    wb = jnp.concatenate([wb_ref[...].astype(f32), jnp.zeros((120, 128), f32)], axis=0).T
-    wsum = jnp.sum(wb, axis=0, keepdims=True)
-    wide = jnp.concatenate([wb, jnp.full((128, 128), 1.0 / 128, f32)], axis=1).astype(bf16)
-    mean_at = jnp.where(iota((128, 128), 1) == 8, 1.0 / 128, 0.0).astype(bf16)
+    wb = wb_ref[...].astype(f32)
+    wsum = jnp.sum(wb, axis=1, keepdims=True)
+    wide = jnp.concatenate([wb, jnp.full((8, 128), 1.0 / 128, f32)], axis=0).astype(bf16)
+    evens = jnp.full((128, 128), 1.0 / 128, f32).astype(bf16)
     loads[0].wait()
 
     def pair_rows(step, _):
         tile = pair[pl.ds(step * 8, 8)].reshape(1024, 128)
-        both = jnp.dot(tile, wide, preferred_element_type=f32)
-        mean = both[:, 128:]
-        centred = tile.astype(f32) - mean
+        centred = tile.astype(f32) - jnp.dot(tile, evens, preferred_element_type=f32)
         square = (centred * centred).astype(bf16)
-        table = both[:, :128] - mean * wsum + jnp.dot(square, mean_at, preferred_element_type=f32)
+        table = lax.dot_general(wide, tile, NT, preferred_element_type=f32)
+        variance = lax.dot_general(evens[0:16], square, NT, preferred_element_type=f32)
+        biases = (table[0:8] - table[8:9] * wsum) * lax.rsqrt(variance[0:8] + epsilon)
         for i in range(8):
-            flipped = table[i * 128 : (i + 1) * 128].T
-            bias = flipped[0:8] * lax.rsqrt(flipped[8:9] + epsilon)
+            bias = biases[:, i * 128 : (i + 1) * 128]
             bt[:, pl.ds(step * 8 + i, 1), :] = bias.reshape(8, 1, 128)
         return 0
 
-    lax.fori_loop(0, 4, pair_rows, 0)
+    lax.fori_loop(0, 6, pair_rows, 0)
 
     pl.semaphore_wait(barrier, 13)
 
@@ -179,9 +178,9 @@
     mask_core = remote(mks, mko, pair_of(c_sem, 0), dev(core=other))
     mask_core.start()
 
-    lax.fori_loop(4, 6, pair_rows, 0)
+    lax.fori_loop(6, 7, pair_rows, 0)
     line_step(wg, w_zl, w_x, 1)
-    lax.fori_loop(6, 8, pair_rows, 0)
+    lax.fori_loop(7, 8, pair_rows, 0)
     btb[...] = bt[...].astype(bf16).reshape(2, 4, T, 128)
     here = pl.ds(pl.multiple_of(core * T, T), T)
     bias_core = remote(btb.at[other], bc.at[:, here], pair_of(c_sem, 1), dev(core=other))

time: 95.7 us -> 95.2 us (level)
  no operation moved by 1% of the time
where the time goes in v5:
time: 95.2 us; the launch traced here: 94.7 us
  Pallas kernels  93 us (98%)
  local copies, waits for them, and re-layouts  1.77 us (2%)
    pallas_call x1, Pallas kernels, body(): pl.pallas_call(kernel, out_shape=jax.ShapeDtypeStruct((S, T, D), bf16), i...  93 us

profile of v5, /device:TPU:1, one launch (start us, length us, event | category | flops | bytes accessed | tf_op | source)
XLA Modules:
  0.0 94.7 jit_solution(8065928086206003362)
XLA Ops:
  0.0 93.0 %pair_attention.1 = bf16[4,64,768]{2,1,0:T(8,128)(2,1)} custom-call(bf16[4,64,768]{2,1,0:T(8,128)(2,1)} %act_h.1, bf16[4,64,768]{2,1,0:T(8,128)(2,1)} %scale_h.1, bf16[4,64,768]{2,1,0:T(8,128)(2,1)} %shift_h.1, bf16[4,64,768]{2,1,0:T(8,128)(2,1)} %gate_h.1, bf16[64,128,128]{2,1,0:T(8,128)(2,1)} %pair_h.1, bf16[8,128]{1,0:T(8,128)(2,1)} %bitcast.1, ...), custom_call_target="tpu_custom_call" | custom-call | flops 2000000000 | bytes 5000000 | tf_op jit(solution)/shard_map/pair_attention/pallas_call | solution.py:528
  93.0 1.8 %copy.14 = bf16[4,64,768]{2,1,0:T(8,128)(2,1)} copy(bf16[4,64,768]{2,1,0:T(8,128)(2,1)} %pair_attention.1) | data formatting | bytes 786432
